TPU v7x, 32 devices: a whole 2x2x4 slice. The times are simulated.
32 devices in a mesh: dp: 8 (over z, y), tensor: 4 (over x, core).
Axes of the slice: x: 2, y: 2, z: 4, core: 2. Of those that a mesh axis runs over, the one named last changes fastest.
Arguments:
- cotangent: bfloat16 [1024, 8192], P('dp'), may hold values from -6 to 6
- inputs: bfloat16 [1024, 8192], P('dp'), may hold values from -6 to 6
- gate_saved: bfloat16 [1024, 14336], P('dp', 'tensor'), may hold values from -6 to 6
- up_saved: bfloat16 [1024, 14336], P('dp', 'tensor'), may hold values from -6 to 6
- gate_weight: bfloat16 [8192, 14336], P('dp', 'tensor'), may hold values from -0.09375 to 0.09375
- up_weight: bfloat16 [8192, 14336], P('dp', 'tensor'), may hold values from -0.0625 to 0.0625
- down_weight: bfloat16 [8192, 14336], P('dp', 'tensor'), may hold values from -0.046875 to 0.046875
- scale_table: float32 [16], replicated, may hold values from 0.5 to 2
- scale_index: int32 [14336], P('tensor'), may hold values from 0 to 15
- clip_mask: int32 [14336], P('tensor'), may hold values 0 or 1
Outputs:
- input_grad: bfloat16 [1024, 8192], P('dp', 'tensor')
- rotation_grad: float32 [8192, 8192], P('dp', 'tensor')
All inputs are finite; a program needn't handle non-finite values. No bound on the sum of `clip_mask` on one device may be relied on, other than what follows from the above.
Results may differ from a plain program's by a relative error of at most 0.012.
Values may be sent and summed in bfloat16 or wider, within the bound.
A program may use at most 384 MiB of HBM per device.

v0:
```python
import math

import jax
import jax.numpy as jnp
from jax import lax
from jax.sharding import PartitionSpec as P

HB = 128


def from_partner(shard, axis, apart):
    return lax.ppermute(shard, axis, [(i, i ^ 1 << apart) for i in range(lax.axis_size(axis))])


def walsh_signs(order_size):
    positions = jnp.arange(order_size, dtype=jnp.int32)
    common = jnp.bitwise_and(positions[:, None], positions[None, :])
    parity = jnp.zeros_like(common)
    shift_count = 0
    while 1 << shift_count < order_size:
        parity = parity + jnp.bitwise_and(jnp.right_shift(common, shift_count), 1)
        shift_count += 1
    return (1 - 2 * (parity % 2)).astype(jnp.float32)


def on_device(
    cotangent,
    inputs,
    gate_saved,
    up_saved,
    gate_weight,
    up_weight,
    down_weight,
    scale_table,
    scale_index,
    clip_mask,
):
    tok_rows = cotangent.shape[0]
    hidden_dev = down_weight.shape[1]
    tensor_count = lax.axis_size("tensor")
    group_count = lax.axis_size("dp")
    cot_cols = lax.all_to_all(cotangent, "dp", split_axis=1, concat_axis=0, tiled=True)
    down_grad = lax.psum_scatter(
        jnp.dot(cot_cols, down_weight, preferred_element_type=jnp.float32),
        "dp",
        scatter_dimension=0,
        tiled=True,
    )
    levels = scale_table.shape[0]
    one_hot = (scale_index[:, None] == jnp.arange(levels, dtype=jnp.int32)[None, :]).astype(
        jnp.float32
    )
    factor = jnp.dot(one_hot, scale_table, precision=lax.Precision.HIGHEST) * clip_mask.astype(
        jnp.float32
    )
    down_grad = down_grad * factor[None, :]
    local = jnp.einsum(
        "nbc,dc->nbd",
        down_grad.reshape(tok_rows, hidden_dev // HB, HB),
        walsh_signs(HB),
        precision=lax.Precision.HIGHEST,
    ).reshape(tok_rows, hidden_dev)
    mixed = local
    my_index = lax.axis_index("tensor")
    for bit_number in range(tensor_count.bit_length() - 1):
        partner = from_partner(mixed, "tensor", bit_number)
        upper = jnp.bitwise_and(jnp.right_shift(my_index, bit_number), 1) == 1
        mixed = jnp.where(upper, partner - mixed, mixed + partner)
    hidden_grad = mixed * (1.0 / math.sqrt(tensor_count * HB))
    gate = gate_saved.astype(jnp.float32)
    up_value = up_saved.astype(jnp.float32)
    sigmoid = jax.nn.sigmoid(gate)
    gate_grad = (hidden_grad * up_value * sigmoid * (1.0 + gate * (1.0 - sigmoid))).astype(
        jnp.bfloat16
    )
    up_grad = (hidden_grad * gate * sigmoid).astype(jnp.bfloat16)
    pieces = lax.all_gather((gate_grad, up_grad), "dp", axis=0, tiled=True)
    first = lax.dot_general(
        pieces[0], gate_weight, (((1,), (1,)), ((), ())), preferred_element_type=jnp.float32
    )
    second = lax.dot_general(
        pieces[1], up_weight, (((1,), (1,)), ((), ())), preferred_element_type=jnp.float32
    )
    feature_part = first + second
    partial_sum = lax.all_to_all(feature_part, "dp", split_axis=0, concat_axis=1, tiled=True)
    input_grad = lax.psum_scatter(partial_sum, "tensor", scatter_dimension=1, tiled=True).astype(
        jnp.bfloat16
    )
    rotation_grad = lax.psum_scatter(
        lax.dot_general(
            inputs, input_grad, (((0,), (0,)), ((), ())), preferred_element_type=jnp.float32
        ).astype(jnp.bfloat16),
        "dp",
        scatter_dimension=0,
        tiled=True,
    ).astype(jnp.float32)
    rotation_grad = rotation_grad * (1.0 / math.sqrt(tok_rows * group_count))
    return (input_grad, rotation_grad)


def solution(mesh):
    placed = (
        P("dp", None),
        P("dp", None),
        P("dp", "tensor"),
        P("dp", "tensor"),
        P("dp", "tensor"),
        P("dp", "tensor"),
        P("dp", "tensor"),
        P(),
        P("tensor"),
        P("tensor"),
    )
    return jax.shard_map(
        on_device,
        mesh=mesh,
        in_specs=placed,
        out_specs=(P("dp", "tensor"), P("dp", "tensor")),
        check_vma=False,
    )
```

profile of v0, /device:TPU:0, one launch (start us, length us, event | category | flops | bytes accessed | tf_op | source)
XLA Modules:
  0.0 1346.8 jit_solution(418624130754866986)
XLA Ops:
  7.2 4.2 copy.34
  11.4 55.6 %all_to_all.38 = bf16[128,8,1024]{0,2,1:T(8,128)(2,1)} all-to-all(bf16[128,8,1024]{0,2,1:T(8,128)(2,1)} %bitcast.29), channel_id=1, replica_groups=mesh['dp'=8,'tensor'=4] {'dp'}, dimensions={1} | all-to-all | bytes 4194304 | tf_op jit(solution)/shard_map/all_to_all | solution.py:42
  67.1 3.9 copy.35
  71.0 13.6 %fusion.34 = f32[1024,3584]{1,0:T(8,128)} fusion(bf16[1024,1024]{1,0:T(8,128)(2,1)} %bitcast.33, bf16[1024,3584]{1,0:T(8,128)(2,1)} %param.16), kind=kOutput, calls=%fused_computation.48 | convolution fusion | flops 7516192768 | bytes 24117248 | tf_op jit(solution)/shard_map/dot_general | solution.py:44
  84.6 0.0 all-gather.5.cloned.1.call-start
  84.7 0.6 copy-done.4
  85.3 0.2 convolution_reduce_fusion
  85.6 234.7 %reduce-scatter.4.cloned.1.call-done = f32[128,3584]{1,0:T(8,128)} async-done(((f32[1024,3584]{1,0:T(8,128)}), f32[128,3584]{1,0:T(8,128)}) %reduce-scatter.4.cloned.1.call-update) | async-done | bytes 1835024 | tf_op jit(solution)/shard_map/reduce_scatter | solution.py:43
  320.3 2.9 broadcast_multiply_fusion
  323.2 2.8 copy.36
  326.0 4.5 fusion.14
  330.5 2.8 copy.38
  333.3 4.1 collective-permute-done
  337.4 3.5 add_select_fusion
  340.9 1.5 collective-permute-start.1
  342.4 40.9 %collective-permute-done.1 = f32[128,3584]{1,0:T(8,128)} collective-permute-done((f32[128,3584]{1,0:T(8,128)}, f32[128,3584]{1,0:T(8,128)}, u32[]{:S(2)}, u32[]{:S(2)}) %collective-permute-start.1) | collective-permute-done | bytes 1835040 | tf_op jit(solution)/shard_map/ppermute | solution.py:12
  383.3 4.7 fusion.5
  388.0 0.7 all-gather.3.cloned.1.call-update
  388.7 0.2 reduce-scatter.6.cloned.1.call-start
  389.0 110.3 %all-gather.5.cloned.1.call-done = bf16[1024,3584]{1,0:T(8,128)(2,1)} async-done(((bf16[128,3584]{1,0:T(8,128)(2,1)}), bf16[1024,3584]{1,0:T(8,128)(2,1)}) %all-gather.5.cloned.1.call-update) | async-done | bytes 7340048 | tf_op jit(solution)/shard_map/all_gather | solution.py:77
  499.2 13.5 %fusion.35 = f32[1024,1024]{1,0:T(8,128)} fusion(bf16[1024,3584]{1,0:T(8,128)(2,1)} %all-gather.5.cloned.1.call-done, bf16[1024,3584]{1,0:T(8,128)(2,1)} %param.15), kind=kOutput, calls=%fused_computation.49 | convolution fusion | flops 7516192768 | bytes 18874368 | tf_op jit(solution)/shard_map/dot_general | solution.py:81
  512.7 98.9 %all-gather.3.cloned.1.call-done = bf16[1024,3584]{1,0:T(8,128)(2,1)} async-done(((bf16[128,3584]{1,0:T(8,128)(2,1)}), bf16[1024,3584]{1,0:T(8,128)(2,1)}) %all-gather.3.cloned.1.call-update) | async-done | bytes 7340048 | tf_op jit(solution)/shard_map/all_gather | solution.py:77
  611.7 12.8 convolution_add_fusion
  624.5 95.9 %all_to_all.39 = f32[8,128,1024]{2,1,0:T(8,128)S(1)} all-to-all(f32[8,128,1024]{2,1,0:T(8,128)S(1)} %bitcast.32), channel_id=1, replica_groups=mesh['dp'=8,'tensor'=4] {'dp'}, dimensions={0} | all-to-all | bytes 8388608 | tf_op jit(solution)/shard_map/all_to_all | solution.py:85
  720.3 2.3 copy.44
  722.7 0.0 reduce-scatter.8.cloned.1.call-start
  722.7 43.6 %reduce-scatter.6.cloned.1.call-done = f32[128,2048]{1,0:T(8,128)} async-done(((f32[128,8192]{1,0:T(8,128)}), f32[128,2048]{1,0:T(8,128)}) %reduce-scatter.6.cloned.1.call-update) | async-done | bytes 1048592 | tf_op jit(solution)/shard_map/reduce_scatter | solution.py:86
  766.3 1.3 convert_element_type.37
  767.6 13.8 %convert_bitcast_fusion = bf16[8192,2048]{0,1:T(8,128)(2,1)} fusion(bf16[128,2048]{1,0:T(8,128)(2,1)S(1)} %convert_element_type.37, bf16[128,8192]{1,0:T(8,128)(2,1)S(1)} %copy-done), kind=kOutput, calls=%fused_computation | convolution fusion | flops 4311744512 | bytes 36175872 | tf_op jit(solution)/shard_map/dot_general | solution.py:90
  781.5 543.1 %reduce-scatter.8.cloned.1.call-done = bf16[1024,2048]{0,1:T(8,128)(2,1)} async-done(((bf16[8192,2048]{0,1:T(8,128)(2,1)}), bf16[1024,2048]{0,1:T(8,128)(2,1)}) %reduce-scatter.8.cloned.1.call-update) | async-done | bytes 4194320 | tf_op jit(solution)/shard_map/reduce_scatter | solution.py:89
  1324.6 6.6 convert_multiply_fusion
  1331.2 9.1 copy.42
  (19 shorter events, 0.2 us)
Async XLA Ops:
  7.2 760.4 %copy-start = (bf16[128,8192]{1,0:T(8,128)(2,1)S(1)}, bf16[128,8192]{1,0:T(8,128)(2,1)}, u32[]{:S(2)}) copy-start(bf16[128,8192]{1,0:T(8,128)(2,1)} %param.11) | copy-start | bytes 6291460
  7.2 313.1 %reduce-scatter.4.cloned.1.call-start = ((), (), s32[]{:S(2)}) async-start(), calls=%async_computation.5 | async-start | bytes 16515072 | tf_op jit(solution)/shard_map/reduce_scatter | solution.py:43
  84.6 0.7 copy-start.4
  84.6 0.7 copy-start.5
  84.6 0.9 copy-start.3
  84.6 414.6 %all-gather.5.cloned.1.call-start = ((), (), s32[]{:S(2)}) async-start(), calls=%async_computation.7 | async-start | bytes 8257536 | tf_op jit(solution)/shard_map/all_gather | solution.py:77
  333.3 4.1 collective-permute-start
  333.3 50.0 %copy-start.2 = (bf16[128,3584]{1,0:T(8,128)(2,1)S(1)}, bf16[128,3584]{1,0:T(8,128)(2,1)}, u32[]{:S(2)}) copy-start(bf16[128,3584]{1,0:T(8,128)(2,1)} %param.12) | copy-start | bytes 2752516
  340.9 42.4 %collective-permute-start.1 = (f32[128,3584]{1,0:T(8,128)}, f32[128,3584]{1,0:T(8,128)}, u32[]{:S(2)}, u32[]{:S(2)}) collective-permute-start(f32[128,3584]{1,0:T(8,128)} %add_select_fusion), channel_id=1, source_target_pairs={{0,2},{1,3},{2,0},{3,1},{4,6},{5,7},{6,4},{7,5},{8,10},{9,11},{10,... | collective-permute-start | bytes 5505032 | tf_op jit(solution)/shard_map/ppermute | solution.py:12
  388.0 223.7 %all-gather.3.cloned.1.call-start = ((), (), s32[]{:S(2)}) async-start(), calls=%async_computation.6 | async-start | bytes 8257536 | tf_op jit(solution)/shard_map/all_gather | solution.py:77
  388.7 377.6 %reduce-scatter.6.cloned.1.call-start = ((), (), s32[]{:S(2)}) async-start(), calls=%async_computation.8 | async-start | bytes 5242880 | tf_op jit(solution)/shard_map/reduce_scatter | solution.py:86
  722.7 601.9 %reduce-scatter.8.cloned.1.call-start = ((), (), s32[]{:S(2)}) async-start(), calls=%async_computation.9 | async-start | bytes 37748736 | tf_op jit(solution)/shard_map/reduce_scatter | solution.py:89
  767.6 13.8 %copy-start.1 = (bf16[128,2048]{1,0:T(8,128)(2,1)}, bf16[128,2048]{1,0:T(8,128)(2,1)S(1)}, u32[]{:S(2)}) copy-start(bf16[128,2048]{1,0:T(8,128)(2,1)S(1)} %convert_element_type.37) | copy-start | bytes 1572868
Sparse Core Ops, SparseCore 0:
  84.8 235.5 reduce-scatter.3
  388.1 111.0 all-gather.4
  501.4 110.1 all-gather.2
  722.8 43.4 reduce-scatter.5
  781.6 542.9 reduce-scatter.7
where the time goes:
time: 1350 us
  waiting for transfers between devices  1080 us (80%)
  blocking collectives  151 us (11%)
  matrix products  58.5 us (4%)
  local copies, waits for them, and re-layouts  25.8 us (2%)
  other arithmetic  19 us (1%)
  between operations  13.9 us (1%)
    reduce_scatter x1, waiting for transfers between devices, on_device(): lax.psum_scatter(lax.dot_general(inputs, input_grad, (((0,), (0,)), ((),...  543 us
    reduce_scatter x1, waiting for transfers between devices, on_device(): lax.psum_scatter(jnp.dot(cot_cols, down_weight, preferred_element_type=jn...  235 us
    all_gather x2, waiting for transfers between devices, on_device(): pieces = lax.all_gather((gate_grad, up_grad), 'dp', axis=0, tiled=True)  209 us
    all_to_all x1, blocking collectives, on_device(): lax.all_to_all(feature_part, 'dp', split_axis=0, concat_axis=1, tiled=True)  95.9 us
    all_to_all x1, blocking collectives, on_device(): lax.all_to_all(cotangent, 'dp', split_axis=1, concat_axis=0, tiled=True)  55.6 us
    ppermute x2, waiting for transfers between devices, from_partner(): lax.ppermute(shard, axis, [(i, i ^ 1 << apart) for i in range(lax.axis_si...  45 us
    reduce_scatter x1, waiting for transfers between devices, on_device(): lax.psum_scatter(partial_sum, 'tensor', scatter_dimension=1, tiled=True)  43.6 us
  transfers between devices with their start and end apart: 7, of which 7 were waited for; matrix products, arithmetic and copies ran while one was open for 1% of the time, Pallas kernels for 0%

commit v1 on v0

--- a/solution.py
+++ b/solution.py
@@ -23,6 +23,26 @@
     return (1 - 2 * (parity % 2)).astype(jnp.float32)
 
 
+def to_owners(summed, my_group, group_count, tensor_count):
+    ratio = group_count // tensor_count
+    blocks = summed.reshape(ratio, summed.shape[0] // ratio, summed.shape[1])
+    position = my_group % ratio
+    arrived = []
+    for turn in range(ratio):
+        pairs = []
+        for i in range(group_count):
+            for t in range(tensor_count):
+                target = (ratio * t + (turn - i) % ratio) * tensor_count + i // ratio
+                pairs.append((i * tensor_count + t, target))
+        block = lax.dynamic_index_in_dim(blocks, (turn - position) % ratio, 0, keepdims=False)
+        arrived.append(lax.ppermute(block, ("dp", "tensor"), pairs))
+    order = jnp.stack(arrived)
+    columns = [
+        lax.dynamic_index_in_dim(order, (c + position) % ratio, 0, keepdims=False) for c in range(ratio)
+    ]
+    return jnp.concatenate(columns, axis=1)
+
+
 def on_device(
     cotangent,
     inputs,
@@ -35,17 +55,34 @@
     scale_index,
     clip_mask,
 ):
-    tok_rows = cotangent.shape[0]
+    tok_rows, width = cotangent.shape
     hidden_dev = down_weight.shape[1]
     tensor_count = lax.axis_size("tensor")
     group_count = lax.axis_size("dp")
-    cot_cols = lax.all_to_all(cotangent, "dp", split_axis=1, concat_axis=0, tiled=True)
+    my_group = lax.axis_index("dp")
+    my_index = lax.axis_index("tensor")
+    feature_rows = width // group_count
+    share = tok_rows // tensor_count
+
+    both = jnp.stack([cotangent, inputs])
+    mine = lax.dynamic_slice_in_dim(both, my_index * share, share, axis=1)
+    turned = lax.all_to_all(
+        mine.reshape(2, share, group_count, feature_rows), "dp", split_axis=2, concat_axis=0, tiled=False
+    )
+
+    def whole(part):
+        gathered = lax.all_gather(part, "tensor", axis=1)
+        return gathered.reshape(group_count * tok_rows, feature_rows)
+
+    cot_cols = whole(turned[:, 0])
+    in_cols = whole(turned[:, 1])
+
     down_grad = lax.psum_scatter(
-        jnp.dot(cot_cols, down_weight, preferred_element_type=jnp.float32),
+        jnp.dot(cot_cols, down_weight, preferred_element_type=jnp.float32).astype(jnp.bfloat16),
         "dp",
         scatter_dimension=0,
         tiled=True,
-    )
+    ).astype(jnp.float32)
     levels = scale_table.shape[0]
     one_hot = (scale_index[:, None] == jnp.arange(levels, dtype=jnp.int32)[None, :]).astype(
         jnp.float32
@@ -54,16 +91,14 @@
         jnp.float32
     )
     down_grad = down_grad * factor[None, :]
-    local = jnp.einsum(
+    mixed = jnp.einsum(
         "nbc,dc->nbd",
         down_grad.reshape(tok_rows, hidden_dev // HB, HB),
         walsh_signs(HB),
         precision=lax.Precision.HIGHEST,
     ).reshape(tok_rows, hidden_dev)
-    mixed = local
-    my_index = lax.axis_index("tensor")
     for bit_number in range(tensor_count.bit_length() - 1):
-        partner = from_partner(mixed, "tensor", bit_number)
+        partner = from_partner(mixed.astype(jnp.bfloat16), "tensor", bit_number).astype(jnp.float32)
         upper = jnp.bitwise_and(jnp.right_shift(my_index, bit_number), 1) == 1
         mixed = jnp.where(upper, partner - mixed, mixed + partner)
     hidden_grad = mixed * (1.0 / math.sqrt(tensor_count * HB))
@@ -81,19 +116,14 @@
     second = lax.dot_general(
         pieces[1], up_weight, (((1,), (1,)), ((), ())), preferred_element_type=jnp.float32
     )
-    feature_part = first + second
-    partial_sum = lax.all_to_all(feature_part, "dp", split_axis=0, concat_axis=1, tiled=True)
-    input_grad = lax.psum_scatter(partial_sum, "tensor", scatter_dimension=1, tiled=True).astype(
+    summed = lax.psum_scatter(first + second, "tensor", scatter_dimension=0, tiled=True).astype(
         jnp.bfloat16
     )
-    rotation_grad = lax.psum_scatter(
-        lax.dot_general(
-            inputs, input_grad, (((0,), (0,)), ((), ())), preferred_element_type=jnp.float32
-        ).astype(jnp.bfloat16),
-        "dp",
-        scatter_dimension=0,
-        tiled=True,
-    ).astype(jnp.float32)
+    input_grad = to_owners(summed, my_group, group_count, tensor_count)
+    all_grad = lax.all_gather(input_grad, "dp", axis=0, tiled=True)
+    rotation_grad = lax.dot_general(
+        in_cols, all_grad, (((0,), (0,)), ((), ())), preferred_element_type=jnp.float32
+    )
     rotation_grad = rotation_grad * (1.0 / math.sqrt(tok_rows * group_count))
     return (input_grad, rotation_grad)
 

time: 1350 us -> 661 us (0.49)
  waiting for transfers between devices: 1080 us -> 533 us
  blocking collectives: 151 us -> 32.8 us
  local copies, waits for them, and re-layouts: 25.8 us -> 10.2 us
    reduce_scatter x2 -> x1, waiting for transfers between devices: 587 us -> 42.2 us  [on_device(): lax.psum_scatter(first + second, 'tensor', scatter_dimension=0, tiled=True)]
    all_gather x0 -> x3, waiting for transfers between devices: none -> 120 us  [the longest x1 77.4 us: on_device(): all_grad = lax.all_gather(input_grad, 'dp', axis=0, tiled=True)]
    all_to_all x2 -> x1, blocking collectives: 151 us -> 32.8 us  [on_device(): lax.all_to_all(mine.reshape(2, share, group_count, feature_rows), 'dp', s...]
    reduce_scatter x1, waiting for transfers between devices: 235 us -> 132 us  [on_device(): lax.psum_scatter(jnp.dot(cot_cols, down_weight, preferred_element_type=jn...]
    ppermute x2, waiting for transfers between devices: 45 us -> 23.9 us  [from_partner(): lax.ppermute(shard, axis, [(i, i ^ 1 << apart) for i in range(lax.axis_si...]
  transfers between devices with their start and end apart: 7 -> 11, of which waited for: 7 -> 10; matrix products, arithmetic and copies ran while one was open for 1% -> 3% of each run, Pallas kernels for 0% -> 0%
where the time goes in v1:
time: 661 us; the launch traced here: 660 us
  waiting for transfers between devices  533 us (81%)
  matrix products  52.7 us (8%)
  blocking collectives  32.8 us (5%)
  between operations  14.3 us (2%)
  other arithmetic  12.8 us (2%)
  local copies, waits for them, and re-layouts  10.2 us (2%)
    all_gather x2, waiting for transfers between devices, on_device(): pieces = lax.all_gather((gate_grad, up_grad), 'dp', axis=0, tiled=True)  209 us
    reduce_scatter x1, waiting for transfers between devices, on_device(): lax.psum_scatter(jnp.dot(cot_cols, down_weight, preferred_element_type=jn...  132 us
    all_gather x1, waiting for transfers between devices, on_device(): all_grad = lax.all_gather(input_grad, 'dp', axis=0, tiled=True)  77.4 us
    all_gather x2, waiting for transfers between devices, whole(): gathered = lax.all_gather(part, 'tensor', axis=1)  42.9 us
    reduce_scatter x1, waiting for transfers between devices, on_device(): lax.psum_scatter(first + second, 'tensor', scatter_dimension=0, tiled=True)  42.2 us
    all_to_all x1, blocking collectives, on_device(): lax.all_to_all(mine.reshape(2, share, group_count, feature_rows), 'dp', s...  32.8 us
    ppermute x2, waiting for transfers between devices, from_partner(): lax.ppermute(shard, axis, [(i, i ^ 1 << apart) for i in range(lax.axis_si...  23.9 us
    dot_general x1, matrix products, on_device(): lax.dot_general(pieces[0], gate_weight, (((1,), (1,)), ((), ())), preferr...  14.1 us
  transfers between devices with their start and end apart: 11, of which 10 were waited for; matrix products, arithmetic and copies ran while one was open for 3% of the time, Pallas kernels for 0%

profile of v1, /device:TPU:0, one launch (start us, length us, event | category | flops | bytes accessed | tf_op | source)
XLA Modules:
  0.0 660.4 jit_solution(13492748501676022949)
XLA Ops:
  7.2 1.3 fusion.12
  9.7 32.8 %all_to_all.15 = bf16[1,2,32,8,1024]{4,2,1,0,3:T(8,128)(2,1)S(1)} all-to-all(bf16[1,2,32,8,1024]{4,2,1,0,3:T(8,128)(2,1)S(1)} %copy.38), channel_id=1, replica_groups=mesh['dp'=8,'tensor'=4] {'dp'}, dimensions={3} | all-to-all | bytes 2097152 | tf_op jit(solution)/shard_map/all_to_all | solution.py:69
  42.5 1.1 slice_bitcast_fusion
  43.7 21.7 %all-gather.6.cloned.1.call-done = bf16[8,4,32,1024]{3,2,0,1:T(8,128)(2,1)} async-done(((bf16[8,1,32,1024]{3,2,0,1:T(8,128)(2,1)}), bf16[8,4,32,1024]{3,2,0,1:T(8,128)(2,1)}) %all-gather.6.cloned.1.call-update) | async-done | bytes 2097168 | tf_op jit(solution)/shard_map/all_gather | solution.py:74
  65.4 1.8 copy.40
  67.2 12.7 %convolution_convert_fusion = bf16[1024,3584]{1,0:T(8,128)(2,1)} fusion(bf16[1024,1024]{1,0:T(8,128)(2,1)S(1)} %bitcast.54, bf16[1024,3584]{1,0:T(8,128)(2,1)} %param.16), kind=kOutput, calls=%fused_computation | convolution fusion | flops 7519862784 | bytes 16777216 | tf_op jit(solution)/shard_map/dot_general | solution.py:81
  80.0 0.6 copy-done.3
  80.9 131.9 %reduce-scatter.3.cloned.1.call-done = bf16[128,3584]{1,0:T(8,128)(2,1)} async-done(((bf16[1024,3584]{1,0:T(8,128)(2,1)}), bf16[128,3584]{1,0:T(8,128)(2,1)}) %reduce-scatter.3.cloned.1.call-update) | async-done | bytes 917520 | tf_op jit(solution)/shard_map/reduce_scatter | solution.py:80
  212.8 2.6 convert_multiply_fusion.2
  215.4 1.8 copy.41
  217.2 3.0 fusion.23
  220.3 1.8 copy.43
  222.1 1.0 convert_element_type.44
  223.1 2.7 collective-permute-done
  225.8 1.2 fusion.11
  227.0 1.5 collective-permute-start.1
  228.4 21.2 %collective-permute-done.1 = bf16[128,3584]{1,0:T(8,128)(2,1)} collective-permute-done((bf16[128,3584]{1,0:T(8,128)(2,1)}, bf16[128,3584]{1,0:T(8,128)(2,1)}, u32[]{:S(2)}, u32[]{:S(2)}) %collective-permute-start.1) | collective-permute-done | bytes 917536 | tf_op jit(solution)/shard_map/ppermute | solution.py:12
  249.7 4.4 fusion.8
  255.0 110.4 %all-gather.10.cloned.1.call-done = bf16[1024,3584]{1,0:T(8,128)(2,1)} async-done(((bf16[128,3584]{1,0:T(8,128)(2,1)}), bf16[1024,3584]{1,0:T(8,128)(2,1)}) %all-gather.10.cloned.1.call-update) | async-done | bytes 7340048 | tf_op jit(solution)/shard_map/all_gather | solution.py:112
  365.4 13.5 %fusion.43 = f32[1024,1024]{1,0:T(8,128)} fusion(bf16[1024,3584]{1,0:T(8,128)(2,1)} %all-gather.10.cloned.1.call-done, bf16[1024,3584]{1,0:T(8,128)(2,1)} %param.15), kind=kOutput, calls=%fused_computation.70 | convolution fusion | flops 7516192768 | bytes 18874368 | tf_op jit(solution)/shard_map/dot_general | solution.py:116
  378.9 98.8 %all-gather.8.cloned.1.call-done = bf16[1024,3584]{1,0:T(8,128)(2,1)} async-done(((bf16[128,3584]{1,0:T(8,128)(2,1)}), bf16[1024,3584]{1,0:T(8,128)(2,1)}) %all-gather.8.cloned.1.call-update) | async-done | bytes 7340048 | tf_op jit(solution)/shard_map/all_gather | solution.py:112
  477.6 14.1 %convolution_add_fusion = f32[1024,1024]{1,0:T(8,128)} fusion(f32[1024,1024]{1,0:T(8,128)} %fusion.43, bf16[1024,3584]{1,0:T(8,128)(2,1)} %all-gather.8.cloned.1.call-done, bf16[1024,3584]{1,0:T(8,128)(2,1)} %param.14), kind=kOutput, calls=%fused_computation.23 | convolution fusion | flops 7517241344 | bytes 23068672 | tf_op jit(solution)/shard_map/dot_general | solution.py:113
  492.5 42.2 %reduce-scatter.5.cloned.1.call-done = f32[256,1024]{1,0:T(8,128)} async-done(((f32[1024,1024]{1,0:T(8,128)}), f32[256,1024]{1,0:T(8,128)}) %reduce-scatter.5.cloned.1.call-update) | async-done | bytes 1048592 | tf_op jit(solution)/shard_map/reduce_scatter | solution.py:119
  534.7 1.3 convert_element_type.52
  536.0 0.7 collective-permute-start.2
  536.7 1.6 collective-permute-start.3
  538.3 4.9 collective-permute-done.3
  543.3 0.8 pad_maximum_fusion
  544.2 21.2 %all-gather.12.cloned.1.call-done = bf16[8,4,32,1024]{3,2,0,1:T(8,128)(2,1)} async-done(((bf16[8,1,32,1024]{3,2,0,1:T(8,128)(2,1)}), bf16[8,4,32,1024]{3,2,0,1:T(8,128)(2,1)}) %all-gather.12.cloned.1.call-update) | async-done | bytes 2097168 | tf_op jit(solution)/shard_map/all_gather | solution.py:74
  565.4 1.8 copy.47
  567.2 77.4 %all-gather.14.cloned.1.call-done = bf16[1024,2048]{1,0:T(8,128)(2,1)} async-done(((bf16[128,2048]{1,0:T(8,128)(2,1)}), bf16[1024,2048]{1,0:T(8,128)(2,1)}) %all-gather.14.cloned.1.call-update) | async-done | bytes 4194320 | tf_op jit(solution)/shard_map/all_gather | solution.py:123
  644.5 9.1 %convolution_multiply_fusion = f32[1024,2048]{1,0:T(8,128)} fusion(bf16[1024,1024]{1,0:T(8,128)(2,1)S(1)} %bitcast.53, bf16[1024,2048]{1,0:T(8,128)(2,1)} %all-gather.14.cloned.1.call-done), kind=kOutput, calls=%fused_computation.1 | convolution fusion | flops 4297064448 | bytes 14680064 | tf_op jit(solution)/shard_map/dot_general | solution.py:124
  (29 shorter events, 3.3 us)
Async XLA Ops:
  7.2 72.9 %copy-start = (f32[16]{0:T(128)S(1)}, f32[16]{0:T(128)}, u32[]{:S(2)}) copy-start(f32[16]{0:T(128)} %param.17) | copy-start | bytes 196
  7.2 58.2 %all-gather.6.cloned.1.call-start = ((), (), s32[]{:S(2)}) async-start(), calls=%async_computation.3 | async-start | bytes 2621440 | tf_op jit(solution)/shard_map/all_gather | solution.py:74
  43.6 169.2 %reduce-scatter.3.cloned.1.call-start = ((), (), s32[]{:S(2)}) async-start(), calls=%async_computation.4 | async-start | bytes 8257536 | tf_op jit(solution)/shard_map/reduce_scatter | solution.py:80
  80.0 0.7 copy-start.3
  80.0 0.9 copy-start.2
  80.0 285.4 %all-gather.10.cloned.1.call-start = ((), (), s32[]{:S(2)}) async-start(), calls=%async_computation.6 | async-start | bytes 8257536 | tf_op jit(solution)/shard_map/all_gather | solution.py:112
  223.1 2.7 collective-permute-start
  227.0 22.7 %collective-permute-start.1 = (bf16[128,3584]{1,0:T(8,128)(2,1)}, bf16[128,3584]{1,0:T(8,128)(2,1)}, u32[]{:S(2)}, u32[]{:S(2)}) collective-permute-start(bf16[128,3584]{1,0:T(8,128)(2,1)} %fusion.11), channel_id=1, source_target_pairs={{0,2},{1,3},{2,0},{3,1},{4,6},{5,7},{6,4},{7,5},{8,10},{9,11},{10,... | collective-permute-start | bytes 2752520 | tf_op jit(solution)/shard_map/ppermute | solution.py:12
  254.2 223.5 %all-gather.8.cloned.1.call-start = ((), (), s32[]{:S(2)}) async-start(), calls=%async_computation.5 | async-start | bytes 8257536 | tf_op jit(solution)/shard_map/all_gather | solution.py:112
  254.7 279.9 %reduce-scatter.5.cloned.1.call-start = ((), (), s32[]{:S(2)}) async-start(), calls=%async_computation.7 | async-start | bytes 5242880 | tf_op jit(solution)/shard_map/reduce_scatter | solution.py:119
  491.8 73.6 %all-gather.12.cloned.1.call-start = ((), (), s32[]{:S(2)}) async-start(), calls=%async_computation.8 | async-start | bytes 2621440 | tf_op jit(solution)/shard_map/all_gather | solution.py:74
  492.4 152.2 %all-gather.14.cloned.1.call-start = ((), (), s32[]{:S(2)}) async-start(), calls=%async_computation.9 | async-start | bytes 4718592 | tf_op jit(solution)/shard_map/all_gather | solution.py:123
  536.0 2.2 collective-permute-start.2
  536.7 6.4 collective-permute-start.3
  644.5 9.1 %copy-start.1 = (f32[16]{0:T(128)S(1)}, f32[16]{0:T(128)}, u32[]{:S(2)}) copy-start(f32[16]{0:T(128)} %param.17) | copy-start | bytes 196
Sparse Core Ops, SparseCore 0:
  43.8 21.5 all-gather.5
  80.1 132.6 reduce-scatter.2
  254.3 111.0 all-gather.9
  367.4 110.1 all-gather.7
  491.9 42.7 reduce-scatter.4
  536.2 29.1 all-gather.11
  568.3 76.2 all-gather.13

commit v2 on v1

--- a/solution.py
+++ b/solution.py
@@ -3,6 +3,8 @@
 import jax
 import jax.numpy as jnp
 from jax import lax
+from jax.experimental import pallas as pl
+from jax.experimental.pallas import tpu as pltpu
 from jax.sharding import PartitionSpec as P
 
 HB = 128
@@ -21,6 +23,205 @@
         parity = parity + jnp.bitwise_and(jnp.right_shift(common, shift_count), 1)
         shift_count += 1
     return (1 - 2 * (parity % 2)).astype(jnp.float32)
+
+
+LINE = 4
+PAIR = 2
+
+
+def spread(x_ref, gathered, send_sem, recv_sem, arrived):
+    chunks = x_ref.shape[0]
+    me = lax.axis_index("dp")
+    z = lax.div(me, PAIR)
+    y = lax.rem(me, PAIR)
+    has_up = z < LINE - 1
+    has_down = z > 0
+    partner = z * PAIR + 1 - y
+    targets = (me + PAIR, me - PAIR, partner)
+
+    barrier = pltpu.get_barrier_semaphore()
+
+    def greet(target):
+        pl.semaphore_signal(
+            barrier, inc=1, device_id={"dp": target}, device_id_type=pl.DeviceIdType.MESH
+        )
+
+    greet(partner)
+    pl.when(has_up)(lambda: greet(targets[0]))
+    pl.when(has_down)(lambda: greet(targets[1]))
+    pl.semaphore_wait(barrier, 1 + has_up.astype(jnp.int32) + has_down.astype(jnp.int32))
+
+    def copy(way, origin, slot, chunk, source):
+        return pltpu.make_async_remote_copy(
+            src_ref=source,
+            dst_ref=gathered.at[slot, chunk],
+            send_sem=send_sem.at[way, origin, chunk],
+            recv_sem=recv_sem.at[slot, chunk],
+            device_id={"dp": targets[way]},
+            device_id_type=pl.DeviceIdType.MESH,
+        )
+
+    def held(slot, chunk):
+        return gathered.at[slot, chunk]
+
+    for chunk in range(chunks):
+        pl.when(has_up)(lambda: copy(0, z, me, chunk, x_ref.at[chunk]).start())
+        pl.when(has_down)(lambda: copy(1, z, me, chunk, x_ref.at[chunk]).start())
+        copy(2, z, me, chunk, x_ref.at[chunk]).start()
+    arrived(me, True)
+
+    def take(slot, chunk):
+        copy(2, z, slot, chunk, held(slot, chunk)).wait_recv()
+
+    for apart in range(1, LINE):
+        for chunk in range(chunks):
+            for way, origin, goes_on in ((0, z - apart, has_up), (1, z + apart, has_down)):
+                slot = origin * PAIR + y
+
+                @pl.when((origin >= 0) & (origin < LINE))
+                def _(way=way, origin=origin, goes_on=goes_on, slot=slot, chunk=chunk):
+                    take(slot, chunk)
+                    pl.when(goes_on)(lambda: copy(way, origin, slot, chunk, held(slot, chunk)).start())
+                    copy(2, origin, slot, chunk, held(slot, chunk)).start()
+
+        for origin in (z - apart, z + apart):
+            pl.when((origin >= 0) & (origin < LINE))(
+                lambda origin=origin: arrived(origin * PAIR + y, False)
+            )
+        if apart == 2:
+            for chunk in range(chunks):
+                take(partner, chunk)
+            arrived(partner, False)
+
+    for apart in range(1, LINE):
+        for origin in (z - apart, z + apart):
+            slot = origin * PAIR + 1 - y
+
+            @pl.when((origin >= 0) & (origin < LINE))
+            def _(slot=slot):
+                for chunk in range(chunks):
+                    take(slot, chunk)
+                arrived(slot, False)
+
+    for chunk in range(chunks):
+        for origin in range(LINE):
+            pl.when(has_up & (origin <= z))(
+                lambda: copy(0, origin, me, chunk, x_ref.at[chunk]).wait_send()
+            )
+            pl.when(has_down & (origin >= z))(
+                lambda: copy(1, origin, me, chunk, x_ref.at[chunk]).wait_send()
+            )
+            copy(2, origin, me, chunk, x_ref.at[chunk]).wait_send()
+
+
+def gather_dot_kernel(
+    x_ref, gate_hbm, up_hbm, out_ref, gathered, weights, weight_sem, send_sem, recv_sem
+):
+    rows = x_ref.shape[1]
+    tile = 256
+    loads = [
+        pltpu.make_async_copy(source, weights.at[k], weight_sem.at[k])
+        for k, source in enumerate((gate_hbm, up_hbm))
+    ]
+    for load in loads:
+        load.start()
+
+    def arrived(slot, own):
+        if own:
+            for load in loads:
+                load.wait()
+        to = pl.ds(pl.multiple_of(slot * rows, rows), rows)
+        source = x_ref if own else gathered.at[slot]
+
+        def step(n, carry):
+            part = pl.ds(pl.multiple_of(n * tile, tile), tile)
+            total = None
+            for k in range(2):
+                product = lax.dot_general(
+                    source[k],
+                    weights[k, part, :],
+                    (((1,), (1,)), ((), ())),
+                    preferred_element_type=jnp.float32,
+                )
+                total = product if total is None else total + product
+            out_ref[to, part] = total
+            return carry
+
+        lax.fori_loop(0, weights.shape[1] // tile, step, 0)
+
+    spread(x_ref, gathered, send_sem, recv_sem, arrived)
+
+
+def gather_dot(grads, gate_weight, up_weight):
+    chunks, rows, depth = grads.shape
+    groups = LINE * PAIR
+    features = gate_weight.shape[0]
+    return pl.pallas_call(
+        gather_dot_kernel,
+        out_shape=jax.ShapeDtypeStruct((groups * rows, features), jnp.float32),
+        in_specs=[
+            pl.BlockSpec(memory_space=pltpu.VMEM),
+            pl.BlockSpec(memory_space=pl.ANY),
+            pl.BlockSpec(memory_space=pl.ANY),
+        ],
+        out_specs=pl.BlockSpec(memory_space=pltpu.VMEM),
+        scratch_shapes=[
+            pltpu.VMEM((groups, chunks, rows, depth), grads.dtype),
+            pltpu.VMEM((2, features, depth), grads.dtype),
+            pltpu.SemaphoreType.DMA((2,)),
+            pltpu.SemaphoreType.DMA((3, LINE, chunks)),
+            pltpu.SemaphoreType.DMA((groups, chunks)),
+        ],
+        compiler_params=pltpu.CompilerParams(
+            collective_id=0, has_side_effects=True, vmem_limit_bytes=52 * 2**20
+        ),
+        cost_estimate=pl.CostEstimate(
+            flops=4 * groups * rows * depth * features,
+            bytes_accessed=4 * features * depth,
+            transcendentals=0,
+        ),
+    )(grads, gate_weight, up_weight)
+
+
+def gather_kernel(x_ref, out_ref, own_sem, send_sem, recv_sem):
+    own_copy = pltpu.make_async_copy(x_ref, out_ref.at[lax.axis_index("dp")], own_sem)
+    own_copy.start()
+    spread(x_ref, out_ref, send_sem, recv_sem, lambda slot, own: None)
+    own_copy.wait()
+
+
+def gather_rows(shard):
+    chunks = 4
+    rows, columns = shard.shape
+    groups = LINE * PAIR
+    gathered = pl.pallas_call(
+        gather_kernel,
+        out_shape=jax.ShapeDtypeStruct((groups, chunks, rows // chunks, columns), shard.dtype),
+        in_specs=[pl.BlockSpec(memory_space=pl.ANY)],
+        out_specs=pl.BlockSpec(memory_space=pl.ANY),
+        scratch_shapes=[
+            pltpu.SemaphoreType.DMA,
+            pltpu.SemaphoreType.DMA((3, LINE, chunks)),
+            pltpu.SemaphoreType.DMA((groups, chunks)),
+        ],
+        compiler_params=pltpu.CompilerParams(collective_id=1, has_side_effects=True),
+        cost_estimate=pl.CostEstimate(
+            flops=0, bytes_accessed=groups * rows * columns * 2, transcendentals=0
+        ),
+    )(shard.reshape(chunks, rows // chunks, columns))
+    return gathered.reshape(groups * rows, columns)
+
+
+def sum_over_tensor(partial, my_index):
+    count = lax.axis_size("tensor")
+    current = partial.reshape(count, partial.shape[0] // count, partial.shape[1])
+    for bit_number in range(count.bit_length() - 1):
+        pairs = current.reshape(current.shape[0] // 2, 2, *current.shape[1:])
+        mine = jnp.bitwise_and(jnp.right_shift(my_index, bit_number), 1)
+        away = lax.dynamic_index_in_dim(pairs, 1 - mine, 1, keepdims=False).astype(jnp.bfloat16)
+        kept = lax.dynamic_index_in_dim(pairs, mine, 1, keepdims=False)
+        current = kept + from_partner(away, "tensor", bit_number).astype(jnp.float32)
+    return current[0]
 
 
 def to_owners(summed, my_group, group_count, tensor_count):
@@ -75,7 +276,13 @@
         return gathered.reshape(group_count * tok_rows, feature_rows)
 
     cot_cols = whole(turned[:, 0])
-    in_cols = whole(turned[:, 1])
+    in_cols = jnp.zeros((group_count, tensor_count, share, feature_rows), inputs.dtype)
+    for turn in range(tensor_count):
+        part = turned[:, 1]
+        if turn:
+            part = lax.ppermute(part, "tensor", [(i, i ^ turn) for i in range(tensor_count)])
+        in_cols = lax.dynamic_update_index_in_dim(in_cols, part, my_index ^ turn, 1)
+    in_cols = in_cols.reshape(group_count * tok_rows, feature_rows)
 
     down_grad = lax.psum_scatter(
         jnp.dot(cot_cols, down_weight, preferred_element_type=jnp.float32).astype(jnp.bfloat16),
@@ -109,18 +316,20 @@
         jnp.bfloat16
     )
     up_grad = (hidden_grad * gate * sigmoid).astype(jnp.bfloat16)
-    pieces = lax.all_gather((gate_grad, up_grad), "dp", axis=0, tiled=True)
-    first = lax.dot_general(
-        pieces[0], gate_weight, (((1,), (1,)), ((), ())), preferred_element_type=jnp.float32
-    )
-    second = lax.dot_general(
-        pieces[1], up_weight, (((1,), (1,)), ((), ())), preferred_element_type=jnp.float32
-    )
-    summed = lax.psum_scatter(first + second, "tensor", scatter_dimension=0, tiled=True).astype(
-        jnp.bfloat16
-    )
+    if group_count == LINE * PAIR:
+        partial = gather_dot(jnp.stack([gate_grad, up_grad]), gate_weight, up_weight)
+    else:
+        pieces = lax.all_gather((gate_grad, up_grad), "dp", axis=0, tiled=True)
+        partial = sum(
+            lax.dot_general(piece, weight, (((1,), (1,)), ((), ())), preferred_element_type=jnp.float32)
+            for piece, weight in zip(pieces, (gate_weight, up_weight))
+        )
+    summed = sum_over_tensor(partial, my_index).astype(jnp.bfloat16)
     input_grad = to_owners(summed, my_group, group_count, tensor_count)
-    all_grad = lax.all_gather(input_grad, "dp", axis=0, tiled=True)
+    if group_count == LINE * PAIR:
+        all_grad = gather_rows(input_grad)
+    else:
+        all_grad = lax.all_gather(input_grad, "dp", axis=0, tiled=True)
     rotation_grad = lax.dot_general(
         in_cols, all_grad, (((0,), (0,)), ((), ())), preferred_element_type=jnp.float32
     )

time: 661 us -> 545 us (0.82)
  waiting for transfers between devices: 533 us -> 246 us
  Pallas kernels: 0 us -> 215 us
  blocking collectives: 32.8 us -> 0 us
  matrix products: 52.7 us -> 25.1 us
  starting transfers between devices: 4.16 us -> 14.6 us
    all_gather x3 -> x0, waiting for transfers between devices: 287 us -> none  [the longest x2 209 us: on_device(): pieces = lax.all_gather((gate_grad, up_grad), 'dp', axis=0, tiled=True)]
    pallas_call x0 -> x2, Pallas kernels: none -> 215 us  [the longest x1 167 us: gather_dot(): pl.pallas_call(gather_dot_kernel, out_shape=jax.ShapeDtypeStruct((groups...]
    reduce_scatter x1 -> x0, waiting for transfers between devices: 42.2 us -> none  [on_device(): lax.psum_scatter(first + second, 'tensor', scatter_dimension=0, tiled=True)]
    all_to_all x1 -> x0, blocking collectives: 32.8 us -> none  [on_device(): lax.all_to_all(mine.reshape(2, share, group_count, feature_rows), 'dp', s...]
    ppermute x0 -> x3, waiting for transfers between devices: none -> 29.6 us  [on_device(): lax.ppermute(part, 'tensor', [(i, i ^ turn) for i in range(tensor_count)])]
    dot_general x2 -> x0, matrix products: 27.6 us -> none  [the longest x1 14.1 us: on_device(): lax.dot_general(pieces[0], gate_weight, (((1,), (1,)), ((), ())), preferr...]
    all_to_all x0 -> x1, waiting for transfers between devices: none -> 25.7 us  [on_device(): lax.all_to_all(mine.reshape(2, share, group_count, feature_rows), 'dp', s...]
    all_gather x2 -> x1, waiting for transfers between devices: 42.9 us -> 21.7 us  [whole(): gathered = lax.all_gather(part, 'tensor', axis=1)]
  transfers between devices with their start and end apart: 11 -> 12, of which waited for: 10 -> 8; matrix products, arithmetic and copies ran while one was open for 3% -> 1% of each run, Pallas kernels for 0% -> 0%
where the time goes in v2:
time: 545 us; the launch traced here: 544 us
  waiting for transfers between devices  246 us (45%)
  Pallas kernels  215 us (39%)
  matrix products  25.1 us (5%)
  local copies, waits for them, and re-layouts  16.5 us (3%)
  starting transfers between devices  14.6 us (3%)
  between operations  14.2 us (3%)
  other arithmetic  13.4 us (2%)
    pallas_call x1, Pallas kernels, gather_dot(): pl.pallas_call(gather_dot_kernel, out_shape=jax.ShapeDtypeStruct((groups...  167 us
    reduce_scatter x1, waiting for transfers between devices, on_device(): lax.psum_scatter(jnp.dot(cot_cols, down_weight, preferred_element_type=jn...  132 us
    pallas_call x1, Pallas kernels, gather_rows(): pl.pallas_call(gather_kernel, out_shape=jax.ShapeDtypeStruct((groups, chu...  48 us
    ppermute x4, waiting for transfers between devices, from_partner(): lax.ppermute(shard, axis, [(i, i ^ 1 << apart) for i in range(lax.axis_si...  36.7 us
    ppermute x3, waiting for transfers between devices, on_device(): lax.ppermute(part, 'tensor', [(i, i ^ turn) for i in range(tensor_count)])  29.6 us
    all_to_all x1, waiting for transfers between devices, on_device(): lax.all_to_all(mine.reshape(2, share, group_count, feature_rows), 'dp', s...  25.7 us
    all_gather x1, waiting for transfers between devices, whole(): gathered = lax.all_gather(part, 'tensor', axis=1)  21.7 us
    dot_general x1, matrix products, on_device(): jnp.dot(cot_cols, down_weight, preferred_element_type=jnp.float32)  12.7 us
  transfers between devices with their start and end apart: 12, of which 8 were waited for; matrix products, arithmetic and copies ran while one was open for 1% of the time, Pallas kernels for 0%

profile of v2, /device:TPU:0, one launch (start us, length us, event | category | flops | bytes accessed | tf_op | source)
XLA Modules:
  0.0 544.1 jit_solution(17391718281771133712)
XLA Ops:
  7.2 1.3 fusion.13
  9.1 1.5 copy.38
  10.6 7.3 %all-to-all-start = ((bf16[1,2,32,8,1024]{4,2,1,0,3:T(8,128)(2,1)}), bf16[1,2,32,8,1024]{4,2,1,0,3:T(8,128)(2,1)S(1)}, u32[]{:S(2)}, u32[]{:S(2)}) async-start(bf16[1,2,32,8,1024]{4,2,1,0,3:T(8,128)(2,1)} %copy.38), calls=%async_computation | async-start | bytes 2097152 | tf_op jit(solution)/shard_map/all_to_all | solution.py:270
  17.9 25.7 %all-to-all-done = bf16[1,2,32,8,1024]{4,2,1,0,3:T(8,128)(2,1)S(1)} async-done(((bf16[1,2,32,8,1024]{4,2,1,0,3:T(8,128)(2,1)}), bf16[1,2,32,8,1024]{4,2,1,0,3:T(8,128)(2,1)S(1)}, u32[]{:S(2)}, u32[]{:S(2)}) %all-to-all-start) | async-done | bytes 1048608 | tf_op jit(solution)/shard_map/all_to_all | solution.py:270
  43.9 1.1 slice_bitcast_fusion.1
  45.0 1.3 copy-done.2
  46.5 21.7 %all-gather.2.cloned.1.call-done = bf16[8,4,32,1024]{3,2,0,1:T(8,128)(2,1)} async-done(((bf16[8,1,32,1024]{3,2,0,1:T(8,128)(2,1)}), bf16[8,4,32,1024]{3,2,0,1:T(8,128)(2,1)}) %all-gather.2.cloned.1.call-update) | async-done | bytes 2097168 | tf_op jit(solution)/shard_map/all_gather | solution.py:275
  68.2 1.8 copy.40
  70.0 12.7 %convolution_convert_fusion = bf16[1024,3584]{1,0:T(8,128)(2,1)} fusion(bf16[1024,1024]{1,0:T(8,128)(2,1)S(1)} %bitcast.79, bf16[1024,3584]{1,0:T(8,128)(2,1)} %param.16), kind=kOutput, calls=%fused_computation.1 | convolution fusion | flops 7519862784 | bytes 16777216 | tf_op jit(solution)/shard_map/dot_general | solution.py:288
  83.7 131.9 %reduce-scatter.2.cloned.1.call-done = bf16[128,3584]{1,0:T(8,128)(2,1)} async-done(((bf16[1024,3584]{1,0:T(8,128)(2,1)}), bf16[128,3584]{1,0:T(8,128)(2,1)}) %reduce-scatter.2.cloned.1.call-update) | async-done | bytes 917520 | tf_op jit(solution)/shard_map/reduce_scatter | solution.py:287
  215.6 2.6 convert_multiply_fusion.2
  218.2 1.8 copy.41
  220.0 3.0 fusion.24
  223.0 1.8 copy.43
  224.8 1.0 convert_element_type.65
  225.9 2.7 collective-permute-done
  228.5 1.2 fusion.11
  229.7 1.5 collective-permute-start.1
  231.2 21.2 %collective-permute-done.1 = bf16[128,3584]{1,0:T(8,128)(2,1)} collective-permute-done((bf16[128,3584]{1,0:T(8,128)(2,1)}, bf16[128,3584]{1,0:T(8,128)(2,1)}, u32[]{:S(2)}, u32[]{:S(2)}) %collective-permute-start.1) | collective-permute-done | bytes 917536 | tf_op jit(solution)/shard_map/ppermute | solution.py:14
  252.4 3.2 fusion.15
  255.8 166.7 %shard_map.113 = f32[1024,1024]{1,0:T(8,128)} custom-call(bf16[2,128,3584]{2,1,0:T(8,128)(2,1)S(1)} %pad_maximum_fusion.x_ref, bf16[1024,3584]{1,0:T(8,128)(2,1)} %gate_hbm.1, bf16[1024,3584]{1,0:T(8,128)(2,1)} %up_hbm.1), custom_call_target="tpu_custom_call" | custom-call | flops 15032385536 | bytes 14680064 | tf_op jit(solution)/shard_map/pallas_call | solution.py:159
  422.6 1.8 fusion.12
  424.9 2.9 collective-permute-done.2
  427.8 1.9 bitcast_add_fusion
  429.8 1.5 collective-permute-start.3
  431.4 1.5 collective-permute-start.7
  432.8 1.9 bitcast_dynamic-update-slice_fusion.2
  434.7 9.9 %collective-permute-done.3 = bf16[1,256,1024]{2,1,0:T(8,128)(2,1)S(1)} collective-permute-done((bf16[1,256,1024]{2,1,0:T(8,128)(2,1)S(1)}, bf16[1,256,1024]{2,1,0:T(8,128)(2,1)S(1)}, u32[]{:S(2)}, u32[]{:S(2)}) %collective-permute-start.3) | collective-permute-done | bytes 524320 | tf_op jit(solution)/shard_map/ppermute | solution.py:14
  444.8 1.5 collective-permute-start.5
  447.0 29.6 %collective-permute-done.7 = bf16[8,32,1024]{2,1,0:T(8,128)(2,1)S(1)} collective-permute-done((bf16[8,32,1024]{2,1,0:T(8,128)(2,1)}, bf16[8,32,1024]{2,1,0:T(8,128)(2,1)S(1)}, u32[]{:S(2)}, u32[]{:S(2)}) %collective-permute-start.7) | collective-permute-done | bytes 524320 | tf_op jit(solution)/shard_map/ppermute | solution.py:283
  479.4 48.0 %shard_map.114 = bf16[8,4,32,2048]{3,2,1,0:T(8,128)(2,1)} custom-call(bf16[4,32,2048]{2,1,0:T(8,128)(2,1)} %pad_maximum_fusion.2.x_ref), custom_call_target="tpu_custom_call" | custom-call | bytes 4194304 | tf_op jit(solution)/shard_map/pallas_call | solution.py:197
  528.2 9.1 %bitcast_multiply_fusion = f32[1024,2048]{1,0:T(8,128)} fusion(bf16[8,4,32,1024]{3,2,1,0:T(8,128)(2,1)S(1)} %copy-done.3, bf16[8,4,32,2048]{3,2,1,0:T(8,128)(2,1)} %shard_map.114), kind=kOutput, calls=%fused_computation | convolution fusion | flops 4297064448 | bytes 14680064 | tf_op jit(solution)/shard_map/dot_general | solution.py:333
  (37 shorter events, 7.1 us)
Async XLA Ops:
  7.2 75.6 %copy-start = (f32[16]{0:T(128)S(1)}, f32[16]{0:T(128)}, u32[]{:S(2)}) copy-start(f32[16]{0:T(128)} %param.17) | copy-start | bytes 196
  10.6 33.0 %all-to-all-start = ((bf16[1,2,32,8,1024]{4,2,1,0,3:T(8,128)(2,1)}), bf16[1,2,32,8,1024]{4,2,1,0,3:T(8,128)(2,1)S(1)}, u32[]{:S(2)}, u32[]{:S(2)}) async-start(bf16[1,2,32,8,1024]{4,2,1,0,3:T(8,128)(2,1)} %copy.38), calls=%async_computation | async-start | bytes 2097152 | tf_op jit(solution)/shard_map/all_to_all | solution.py:270
  17.9 50.3 %all-gather.2.cloned.1.call-start = ((), (), s32[]{:S(2)}) async-start(), calls=%async_computation.2 | async-start | bytes 2621440 | tf_op jit(solution)/shard_map/all_gather | solution.py:275
  45.0 1.3 copy-start.2
  46.4 169.2 %reduce-scatter.2.cloned.1.call-start = ((), (), s32[]{:S(2)}) async-start(), calls=%async_computation.3 | async-start | bytes 8257536 | tf_op jit(solution)/shard_map/reduce_scatter | solution.py:287
  82.7 0.7 copy-start.5
  82.7 0.9 copy-start.4
  225.9 2.7 collective-permute-start
  229.7 22.7 %collective-permute-start.1 = (bf16[128,3584]{1,0:T(8,128)(2,1)}, bf16[128,3584]{1,0:T(8,128)(2,1)}, u32[]{:S(2)}, u32[]{:S(2)}) collective-permute-start(bf16[128,3584]{1,0:T(8,128)(2,1)} %fusion.11), channel_id=1, source_target_pairs={{0,2},{1,3},{2,0},{3,1},{4,6},{5,7},{6,4},{7,5},{8,10},{9,11},{10,... | collective-permute-start | bytes 2752520 | tf_op jit(solution)/shard_map/ppermute | solution.py:14
  424.3 3.4 collective-permute-start.2
  424.4 8.4 %collective-permute-start.6 = (bf16[8,32,1024]{2,1,0:T(8,128)(2,1)}, bf16[8,32,1024]{2,1,0:T(8,128)(2,1)}, u32[]{:S(2)}, u32[]{:S(2)}) collective-permute-start(bf16[8,32,1024]{2,1,0:T(8,128)(2,1)} %get-tuple-element.4), channel_id=1, source_target_pairs={{0,1},{1,0},{2,3},{3,2},{4,5},{5,4},{6,7},{7,6},{8,9},{9,8},{10,11... | collective-permute-start | bytes 1572872 | tf_op jit(solution)/shard_map/ppermute | solution.py:283
  429.8 14.8 %collective-permute-start.3 = (bf16[1,256,1024]{2,1,0:T(8,128)(2,1)S(1)}, bf16[1,256,1024]{2,1,0:T(8,128)(2,1)S(1)}, u32[]{:S(2)}, u32[]{:S(2)}) collective-permute-start(bf16[1,256,1024]{2,1,0:T(8,128)(2,1)S(1)} %dynamic-slice_convert_fusion.1), channel_id=1, source_target_pairs={{0,2},{1,3},{2,0},{3,1},{4,6},{5,7},{6,4},{7,5},{8,10},{9,11},{10,... | collective-permute-start | bytes 1572872 | tf_op jit(solution)/shard_map/ppermute | solution.py:14
  431.3 46.1 %collective-permute-start.8 = (bf16[8,32,1024]{2,1,0:T(8,128)(2,1)}, bf16[8,32,1024]{2,1,0:T(8,128)(2,1)S(1)}, u32[]{:S(2)}, u32[]{:S(2)}) collective-permute-start(bf16[8,32,1024]{2,1,0:T(8,128)(2,1)} %get-tuple-element.4), channel_id=1, source_target_pairs={{0,3},{1,2},{2,1},{3,0},{4,7},{5,6},{6,5},{7,4},{8,11},{9,10},{10,... | collective-permute-start | bytes 1572872 | tf_op jit(solution)/shard_map/ppermute | solution.py:283
  431.4 45.3 %collective-permute-start.7 = (bf16[8,32,1024]{2,1,0:T(8,128)(2,1)}, bf16[8,32,1024]{2,1,0:T(8,128)(2,1)S(1)}, u32[]{:S(2)}, u32[]{:S(2)}) collective-permute-start(bf16[8,32,1024]{2,1,0:T(8,128)(2,1)} %get-tuple-element.4), channel_id=1, source_target_pairs={{0,2},{1,3},{2,0},{3,1},{4,6},{5,7},{6,4},{7,5},{8,10},{9,11},{10,... | collective-permute-start | bytes 1572872 | tf_op jit(solution)/shard_map/ppermute | solution.py:283
  444.8 33.5 %collective-permute-start.5 = (bf16[128,1024]{1,0:T(8,128)(2,1)S(1)}, bf16[128,1024]{1,0:T(8,128)(2,1)S(1)}, u32[]{:S(2)}, u32[]{:S(2)}) collective-permute-start(bf16[128,1024]{1,0:T(8,128)(2,1)S(1)} %get-tuple-element.9), channel_id=1, source_target_pairs={{0,4},{1,12},{2,20},{3,28},{4,0},{5,8},{6,16},{7,24},{8,5},{9,13},... | collective-permute-start | bytes 786440 | tf_op jit(solution)/shard_map/ppermute | solution.py:239
  446.4 32.0 %collective-permute-start.4 = (bf16[128,1024]{1,0:T(8,128)(2,1)S(1)}, bf16[128,1024]{1,0:T(8,128)(2,1)S(1)}, u32[]{:S(2)}, u32[]{:S(2)}) collective-permute-start(bf16[128,1024]{1,0:T(8,128)(2,1)S(1)} %get-tuple-element.10), channel_id=1, source_target_pairs={{0,0},{1,8},{2,16},{3,24},{4,4},{5,12},{6,20},{7,28},{8,1},{9,9},{... | collective-permute-start | bytes 786440 | tf_op jit(solution)/shard_map/ppermute | solution.py:239
  479.4 48.9 %copy-start.3 = (bf16[8,4,32,1024]{3,2,1,0:T(8,128)(2,1)S(1)}, bf16[8,4,32,1024]{3,2,1,0:T(8,128)(2,1)}, u32[]{:S(2)}) copy-start(bf16[8,4,32,1024]{3,2,1,0:T(8,128)(2,1)} %bitcast_dynamic-update-slice_fusion) | copy-start | bytes 6291460
  528.2 9.1 %copy-start.1 = (f32[16]{0:T(128)S(1)}, f32[16]{0:T(128)}, u32[]{:S(2)}) copy-start(f32[16]{0:T(128)} %param.17) | copy-start | bytes 196
Sparse Core Ops, SparseCore 0:
  46.5 21.5 all-gather.1
  82.9 132.6 reduce-scatter.1

commit v3 on v2

--- a/solution.py
+++ b/solution.py
@@ -290,6 +290,7 @@
         scatter_dimension=0,
         tiled=True,
     ).astype(jnp.float32)
+    down_grad, in_cols = lax.optimization_barrier((down_grad, in_cols))
     levels = scale_table.shape[0]
     one_hot = (scale_index[:, None] == jnp.arange(levels, dtype=jnp.int32)[None, :]).astype(
         jnp.float32

time: 545 us -> 532 us (0.976)
  waiting for transfers between devices: 246 us -> 195 us
  blocking collectives: 0 us -> 32.8 us
  Pallas kernels: 215 us -> 226 us
  starting transfers between devices: 14.6 us -> 7.32 us
    all_to_all x0 -> x1, blocking collectives: none -> 32.8 us  [on_device(): lax.all_to_all(mine.reshape(2, share, group_count, feature_rows), 'dp', s...]
    all_to_all x1 -> x0, waiting for transfers between devices: 25.7 us -> none  [on_device(): lax.all_to_all(mine.reshape(2, share, group_count, feature_rows), 'dp', s...]
    reduce_scatter x1, waiting for transfers between devices: 132 us -> 107 us  [on_device(): lax.psum_scatter(jnp.dot(cot_cols, down_weight, preferred_element_type=jn...]
    pallas_call x1, Pallas kernels: 48 us -> 59.4 us  [gather_rows(): pl.pallas_call(gather_kernel, out_shape=jax.ShapeDtypeStruct((groups, chu...]
    ppermute x3, waiting for transfers between devices: 29.6 us -> 20.7 us  [on_device(): lax.ppermute(part, 'tensor', [(i, i ^ turn) for i in range(tensor_count)])]
    all_to_all x1 -> x0, starting transfers between devices: 7.28 us -> none  [on_device(): lax.all_to_all(mine.reshape(2, share, group_count, feature_rows), 'dp', s...]
    ppermute x2, waiting for transfers between devices: 0.01 us -> 6.82 us  [to_owners(): arrived.append(lax.ppermute(block, ('dp', 'tensor'), pairs))]
  transfers between devices with their start and end apart: 12 -> 11, of which waited for: 8 -> 9; matrix products, arithmetic and copies ran while one was open for 1% -> 1% of each run, Pallas kernels for 0% -> 0%
where the time goes in v3:
time: 532 us; the launch traced here: 527 us
  Pallas kernels  226 us (42%)
  waiting for transfers between devices  195 us (37%)
  blocking collectives  32.8 us (6%)
  matrix products  26.6 us (5%)
  between operations  14.3 us (3%)
  local copies, waits for them, and re-layouts  12.5 us (2%)
  other arithmetic  12.3 us (2%)
  starting transfers between devices  7.32 us (1%)
    pallas_call x1, Pallas kernels, gather_dot(): pl.pallas_call(gather_dot_kernel, out_shape=jax.ShapeDtypeStruct((groups...  167 us
    reduce_scatter x1, waiting for transfers between devices, on_device(): lax.psum_scatter(jnp.dot(cot_cols, down_weight, preferred_element_type=jn...  107 us
    pallas_call x1, Pallas kernels, gather_rows(): pl.pallas_call(gather_kernel, out_shape=jax.ShapeDtypeStruct((groups, chu...  59.4 us
    ppermute x4, waiting for transfers between devices, from_partner(): lax.ppermute(shard, axis, [(i, i ^ 1 << apart) for i in range(lax.axis_si...  39 us
    all_to_all x1, blocking collectives, on_device(): lax.all_to_all(mine.reshape(2, share, group_count, feature_rows), 'dp', s...  32.8 us
    all_gather x1, waiting for transfers between devices, whole(): gathered = lax.all_gather(part, 'tensor', axis=1)  21.7 us
    ppermute x3, waiting for transfers between devices, on_device(): lax.ppermute(part, 'tensor', [(i, i ^ turn) for i in range(tensor_count)])  20.7 us
    dot_general x1, matrix products, on_device(): jnp.dot(cot_cols, down_weight, preferred_element_type=jnp.float32)  12.7 us
  transfers between devices with their start and end apart: 11, of which 9 were waited for; matrix products, arithmetic and copies ran while one was open for 1% of the time, Pallas kernels for 0%

profile of v3, /device:TPU:0, one launch (start us, length us, event | category | flops | bytes accessed | tf_op | source)
XLA Modules:
  0.0 527.2 jit_solution(7629703976522142235)
XLA Ops:
  7.2 1.3 fusion.13
  9.7 32.8 %all_to_all.15 = bf16[1,2,32,8,1024]{4,2,1,0,3:T(8,128)(2,1)S(1)} all-to-all(bf16[1,2,32,8,1024]{4,2,1,0,3:T(8,128)(2,1)S(1)} %copy.43), channel_id=1, replica_groups=mesh['dp'=8,'tensor'=4] {'dp'}, dimensions={3} | all-to-all | bytes 2097152 | tf_op jit(solution)/shard_map/all_to_all | solution.py:270
  42.6 1.1 slice_bitcast_fusion
  43.8 21.7 %all-gather.2.cloned.1.call-done = bf16[8,4,32,1024]{3,2,0,1:T(8,128)(2,1)} async-done(((bf16[8,1,32,1024]{3,2,0,1:T(8,128)(2,1)}), bf16[8,4,32,1024]{3,2,0,1:T(8,128)(2,1)}) %all-gather.2.cloned.1.call-update) | async-done | bytes 2097168 | tf_op jit(solution)/shard_map/all_gather | solution.py:275
  65.5 1.8 copy.45
  67.3 12.7 %convolution_convert_fusion = bf16[1024,3584]{1,0:T(8,128)(2,1)} fusion(bf16[1024,1024]{1,0:T(8,128)(2,1)S(1)} %bitcast.80, bf16[1024,3584]{1,0:T(8,128)(2,1)} %param.16), kind=kOutput, calls=%fused_computation | convolution fusion | flops 7519862784 | bytes 16777216 | tf_op jit(solution)/shard_map/dot_general | solution.py:288
  81.4 1.3 collective-permute-start.2
  83.0 1.1 bitcast_dynamic-update-slice_fusion.1
  84.1 12.1 %collective-permute-done.1 = bf16[8,32,1024]{2,1,0:T(8,128)(2,1)} collective-permute-done((bf16[8,32,1024]{2,1,0:T(8,128)(2,1)}, bf16[8,32,1024]{2,1,0:T(8,128)(2,1)}, u32[]{:S(2)}, u32[]{:S(2)}) %collective-permute-start.1) | collective-permute-done | bytes 524320 | tf_op jit(solution)/shard_map/ppermute | solution.py:283
  96.1 1.1 bitcast_dynamic-update-slice_fusion
  97.2 8.6 %collective-permute-done.2 = bf16[8,32,1024]{2,1,0:T(8,128)(2,1)S(1)} collective-permute-done((bf16[8,32,1024]{2,1,0:T(8,128)(2,1)}, bf16[8,32,1024]{2,1,0:T(8,128)(2,1)S(1)}, u32[]{:S(2)}, u32[]{:S(2)}) %collective-permute-start.2) | collective-permute-done | bytes 524320 | tf_op jit(solution)/shard_map/ppermute | solution.py:283
  105.9 107.0 %reduce-scatter.2.cloned.1.call-done = bf16[128,3584]{1,0:T(8,128)(2,1)} async-done(((bf16[1024,3584]{1,0:T(8,128)(2,1)}), bf16[128,3584]{1,0:T(8,128)(2,1)}) %reduce-scatter.2.cloned.1.call-update) | async-done | bytes 917520 | tf_op jit(solution)/shard_map/reduce_scatter | solution.py:287
  212.9 1.4 convert_element_type.62
  214.4 1.7 copy.49
  216.1 4.6 fusion.24
  220.7 1.8 copy.51
  222.5 1.0 convert_element_type.65
  223.5 2.7 collective-permute-done.3
  226.2 1.2 fusion.11
  227.4 1.5 collective-permute-start.4
  228.9 21.2 %collective-permute-done.4 = bf16[128,3584]{1,0:T(8,128)(2,1)} collective-permute-done((bf16[128,3584]{1,0:T(8,128)(2,1)}, bf16[128,3584]{1,0:T(8,128)(2,1)}, u32[]{:S(2)}, u32[]{:S(2)}) %collective-permute-start.4) | collective-permute-done | bytes 917536 | tf_op jit(solution)/shard_map/ppermute | solution.py:14
  250.1 3.2 fusion.15
  253.5 166.7 %shard_map.113 = f32[1024,1024]{1,0:T(8,128)} custom-call(bf16[2,128,3584]{2,1,0:T(8,128)(2,1)S(1)} %pad_maximum_fusion.x_ref, bf16[1024,3584]{1,0:T(8,128)(2,1)} %gate_hbm.1, bf16[1024,3584]{1,0:T(8,128)(2,1)} %up_hbm.1), custom_call_target="tpu_custom_call" | custom-call | flops 15032385536 | bytes 14680064 | tf_op jit(solution)/shard_map/pallas_call | solution.py:159
  420.2 1.8 fusion.12
  422.1 2.6 collective-permute-done.5
  424.7 1.9 bitcast_add_fusion
  426.7 1.6 collective-permute-start.6
  428.3 12.5 %collective-permute-done.6 = bf16[1,256,1024]{2,1,0:T(8,128)(2,1)S(1)} collective-permute-done((bf16[1,256,1024]{2,1,0:T(8,128)(2,1)S(1)}, bf16[1,256,1024]{2,1,0:T(8,128)(2,1)S(1)}, u32[]{:S(2)}, u32[]{:S(2)}) %collective-permute-start.6) | collective-permute-done | bytes 524320 | tf_op jit(solution)/shard_map/ppermute | solution.py:14
  441.0 1.5 collective-permute-start.8
  443.2 6.8 %collective-permute-done.8 = bf16[128,1024]{1,0:T(8,128)(2,1)S(1)} collective-permute-done((bf16[128,1024]{1,0:T(8,128)(2,1)S(1)}, bf16[128,1024]{1,0:T(8,128)(2,1)S(1)}, u32[]{:S(2)}, u32[]{:S(2)}) %collective-permute-start.8) | collective-permute-done | bytes 262176 | tf_op jit(solution)/shard_map/ppermute | solution.py:239
  451.1 59.4 %shard_map.114 = bf16[8,4,32,2048]{3,2,1,0:T(8,128)(2,1)} custom-call(bf16[4,32,2048]{2,1,0:T(8,128)(2,1)} %pad_maximum_fusion.2.x_ref), custom_call_target="tpu_custom_call" | custom-call | bytes 4194304 | tf_op jit(solution)/shard_map/pallas_call | solution.py:197
  511.3 9.1 %convolution_multiply_fusion = f32[1024,2048]{1,0:T(8,128)} fusion(bf16[1024,1024]{1,0:T(8,128)(2,1)S(1)} %bitcast.77, bf16[1024,2048]{1,0:T(8,128)(2,1)} %bitcast.67), kind=kOutput, calls=%fused_computation.1 | convolution fusion | flops 4297064448 | bytes 14680064 | tf_op jit(solution)/shard_map/dot_general | solution.py:334
  (39 shorter events, 6.3 us)
Async XLA Ops:
  7.2 73.2 %copy-start = (f32[16]{0:T(128)S(1)}, f32[16]{0:T(128)}, u32[]{:S(2)}) copy-start(f32[16]{0:T(128)} %param.17) | copy-start | bytes 196
  7.2 58.3 %all-gather.2.cloned.1.call-start = ((), (), s32[]{:S(2)}) async-start(), calls=%async_computation.2 | async-start | bytes 2621440 | tf_op jit(solution)/shard_map/all_gather | solution.py:275
  43.7 169.2 %reduce-scatter.2.cloned.1.call-start = ((), (), s32[]{:S(2)}) async-start(), calls=%async_computation.3 | async-start | bytes 8257536 | tf_op jit(solution)/shard_map/reduce_scatter | solution.py:287
  80.1 0.7 copy-start.5
  80.1 1.3 copy-start.4
  80.1 2.9 collective-permute-start
  81.0 15.2 %collective-permute-start.1 = (bf16[8,32,1024]{2,1,0:T(8,128)(2,1)}, bf16[8,32,1024]{2,1,0:T(8,128)(2,1)}, u32[]{:S(2)}, u32[]{:S(2)}) collective-permute-start(bf16[8,32,1024]{2,1,0:T(8,128)(2,1)} %get-tuple-element.8), channel_id=1, source_target_pairs={{0,2},{1,3},{2,0},{3,1},{4,6},{5,7},{6,4},{7,5},{8,10},{9,11},{10,... | collective-permute-start | bytes 1572872 | tf_op jit(solution)/shard_map/ppermute | solution.py:283
  81.4 24.5 %collective-permute-start.2 = (bf16[8,32,1024]{2,1,0:T(8,128)(2,1)}, bf16[8,32,1024]{2,1,0:T(8,128)(2,1)S(1)}, u32[]{:S(2)}, u32[]{:S(2)}) collective-permute-start(bf16[8,32,1024]{2,1,0:T(8,128)(2,1)} %get-tuple-element.8), channel_id=1, source_target_pairs={{0,3},{1,2},{2,1},{3,0},{4,7},{5,6},{6,5},{7,4},{8,11},{9,10},{10,... | collective-permute-start | bytes 1572872 | tf_op jit(solution)/shard_map/ppermute | solution.py:283
  105.9 108.3 %copy-start.2 = (bf16[8,4,32,1024]{3,2,1,0:T(8,128)(2,1)}, bf16[8,4,32,1024]{3,2,1,0:T(8,128)(2,1)S(1)}, u32[]{:S(2)}) copy-start(bf16[8,4,32,1024]{3,2,1,0:T(8,128)(2,1)S(1)} %bitcast_dynamic-update-slice_fusion.2) | copy-start | bytes 6291460
  223.5 2.7 collective-permute-start.3
  227.4 22.7 %collective-permute-start.4 = (bf16[128,3584]{1,0:T(8,128)(2,1)}, bf16[128,3584]{1,0:T(8,128)(2,1)}, u32[]{:S(2)}, u32[]{:S(2)}) collective-permute-start(bf16[128,3584]{1,0:T(8,128)(2,1)} %fusion.11), channel_id=1, source_target_pairs={{0,2},{1,3},{2,0},{3,1},{4,6},{5,7},{6,4},{7,5},{8,10},{9,11},{10,... | collective-permute-start | bytes 2752520 | tf_op jit(solution)/shard_map/ppermute | solution.py:14
  422.0 2.7 collective-permute-start.5
  426.7 14.0 %collective-permute-start.6 = (bf16[1,256,1024]{2,1,0:T(8,128)(2,1)S(1)}, bf16[1,256,1024]{2,1,0:T(8,128)(2,1)S(1)}, u32[]{:S(2)}, u32[]{:S(2)}) collective-permute-start(bf16[1,256,1024]{2,1,0:T(8,128)(2,1)S(1)} %dynamic-slice_convert_fusion.1), channel_id=1, source_target_pairs={{0,2},{1,3},{2,0},{3,1},{4,6},{5,7},{6,4},{7,5},{8,10},{9,11},{10,... | collective-permute-start | bytes 1572872 | tf_op jit(solution)/shard_map/ppermute | solution.py:14
  441.0 9.1 %collective-permute-start.8 = (bf16[128,1024]{1,0:T(8,128)(2,1)S(1)}, bf16[128,1024]{1,0:T(8,128)(2,1)S(1)}, u32[]{:S(2)}, u32[]{:S(2)}) collective-permute-start(bf16[128,1024]{1,0:T(8,128)(2,1)S(1)} %get-tuple-element.12), channel_id=1, source_target_pairs={{0,4},{1,12},{2,20},{3,28},{4,0},{5,8},{6,16},{7,24},{8,5},{9,13},... | collective-permute-start | bytes 786440 | tf_op jit(solution)/shard_map/ppermute | solution.py:239
  442.5 7.5 %collective-permute-start.7 = (bf16[128,1024]{1,0:T(8,128)(2,1)S(1)}, bf16[128,1024]{1,0:T(8,128)(2,1)S(1)}, u32[]{:S(2)}, u32[]{:S(2)}) collective-permute-start(bf16[128,1024]{1,0:T(8,128)(2,1)S(1)} %get-tuple-element.13), channel_id=1, source_target_pairs={{0,0},{1,8},{2,16},{3,24},{4,4},{5,12},{6,20},{7,28},{8,1},{9,9},{... | collective-permute-start | bytes 786440 | tf_op jit(solution)/shard_map/ppermute | solution.py:239
  451.1 60.2 %copy-start.3 = (bf16[8,4,32,1024]{3,2,1,0:T(8,128)(2,1)S(1)}, bf16[8,4,32,1024]{3,2,1,0:T(8,128)(2,1)}, u32[]{:S(2)}) copy-start(bf16[8,4,32,1024]{3,2,1,0:T(8,128)(2,1)} %copy-done.2) | copy-start | bytes 6291460
  511.3 9.1 %copy-start.1 = (f32[16]{0:T(128)S(1)}, f32[16]{0:T(128)}, u32[]{:S(2)}) copy-start(f32[16]{0:T(128)} %param.17) | copy-start | bytes 196
Sparse Core Ops, SparseCore 0:
  43.9 21.5 all-gather.1
  80.2 132.6 reduce-scatter.1
